TPU v7x, 256 devices: a whole 4x4x8 slice. The times are simulated.
256 devices in a mesh: series: 16 (over z, core), tm: 16 (over y, x).
Axes of the slice: x: 4, y: 4, z: 8, core: 2. Of those that a mesh axis runs over, the one named last changes fastest.
Arguments:
- traffic: bfloat16 [32768, 32768], P('series', 'tm'), may hold values from -170 to 170
- sketch: float32 [32768, 64], P('tm'), may hold values from -0.03125 to 0.03125
Outputs:
- first: float32 [32768, 64], P('series')
- back_out: float32 [32768, 64], P('tm')
- basis: float32 [32768, 64], P('series')
- projection: float32 [64, 32768], P(None, 'tm')
All inputs are finite; a program needn't handle non-finite values.
Results may differ from a plain program's by a relative error of at most 0.0003.
Values sent between devices are 32-bit elements; how exact they have to be, the bound alone decides.
A program may use at most 64 MiB of HBM per device.

v0:
```python
import jax
import jax.numpy as jnp
from jax import lax
from jax.sharding import PartitionSpec as P


def gram_of(tall):
    return jnp.dot(
        tall.T, tall, precision=lax.Precision.HIGHEST, preferred_element_type=jnp.float32
    )


def right_apply(tile, panel):
    return jnp.dot(tile, panel, precision=lax.Precision.HIGHEST, preferred_element_type=jnp.float32)


def left_apply(tile, panel):
    return lax.dot_general(
        tile,
        panel,
        (((0,), (0,)), ((), ())),
        precision=lax.Precision.HIGHEST,
        preferred_element_type=jnp.float32,
    )


def solve_right(lower, tall):
    return jax.scipy.linalg.solve_triangular(lower, tall.T, lower=True).T


def local(traffic, sketch):
    rows_total = traffic.shape[0] * lax.axis_size("series")
    cols_total = traffic.shape[1] * lax.axis_size("tm")
    sampled = lax.psum(right_apply(traffic, sketch), "tm")
    gram_one = lax.psum(gram_of(sampled), "series")
    first_basis = solve_right(jnp.linalg.cholesky(gram_one), sampled)
    back = lax.psum(left_apply(traffic, first_basis), "series")
    gram_two = lax.psum(gram_of(back), "tm")
    back_basis = solve_right(jnp.linalg.cholesky(gram_two), back)
    forward = lax.psum(right_apply(traffic, back_basis), "tm")
    gram_three = lax.psum(gram_of(forward), "series")
    final_basis = solve_right(jnp.linalg.cholesky(gram_three), forward)
    projection = lax.psum(left_apply(final_basis, traffic), "series")
    first = jnp.sqrt(jnp.float32(rows_total)) * first_basis
    back_out = jnp.sqrt(jnp.float32(cols_total)) * back_basis
    basis = jnp.sqrt(jnp.float32(rows_total)) * final_basis
    return (first, back_out, basis, projection)


def solution(mesh):
    in_specs = (P("series", "tm"), P("tm", None))
    out_specs = (P("series", None), P("tm", None), P("series", None), P(None, "tm"))
    return jax.shard_map(local, mesh=mesh, in_specs=in_specs, out_specs=out_specs, check_vma=False)
```

profile of v0, /device:TPU:1, one launch (start us, length us, event | category | flops | bytes accessed | tf_op | source)
XLA Modules:
  0.0 674.5 jit_solution(16618687614881082257)
XLA Ops:
  7.2 0.0 copy-start
  7.2 0.0 all-reduce.5.cloned.1.call-start
  7.2 1.0 copy-done
  8.2 10.8 %fusion.15 = f32[2048,64]{0,1:T(8,128)} fusion(bf16[2048,2048]{1,0:T(8,128)(2,1)} %param.5, f32[2048,64]{0,1:T(8,128)S(1)} %copy-done), kind=kOutput, calls=%fused_computation.34 | convolution fusion | flops 3221225472 | bytes 9437184 | tf_op jit(solution)/shard_map/dot_general | solution.py:14
  19.0 0.0 all-reduce.5.cloned.1.call-update
  19.0 0.0 all-reduce.7.cloned.1.call-start
  19.1 97.9 %all-reduce.5.cloned.1.call-done = f32[2048,64]{0,1:T(8,128)} async-done(((f32[2048,64]{0,1:T(8,128)}), f32[2048,64]{0,1:T(8,128)}) %all-reduce.5.cloned.1.call-update) | async-done | bytes 524304 | tf_op jit(solution)/shard_map/psum | solution.py:34
  117.0 1.8 fusion.16
  118.7 45.5 %psum.50 = f32[64,64]{0,1:T(8,128)S(1)} all-reduce(f32[64,64]{0,1:T(8,128)S(1)} %fusion.16), channel_id=1, replica_groups=mesh['series'=16,'tm'=16] {'series'}, use_global_device_ids=true, to_apply=%region_1.0 | all-reduce | flops 4096 | bytes 32768 | tf_op jit(solution)/shard_map/psum | solution.py:35
  164.2 0.1 copy.7
  164.3 5.8 cholesky.59
  170.2 0.6 compare_reduce_fusion.2
  170.8 0.7 fusion.6
  171.5 4.9 custom-call.7
  176.4 1.7 fusion.4
  178.1 7.6 %convolution_bitcast_fusion.1 = f32[2048,64]{0,1:T(8,128)} fusion(f32[64,2048]{1,0:T(8,128)S(1)} %fusion.4, bf16[2048,2048]{1,0:T(8,128)(2,1)} %param.5), kind=kOutput, calls=%fused_computation.1 | convolution fusion | flops 3221225472 | bytes 9437184 | tf_op jit(solution)/shard_map/dot_general | solution.py:18
  185.7 0.0 all-reduce.7.cloned.1.call-update
  185.7 0.0 all-reduce.9.cloned.1.call-start
  185.8 110.7 %all-reduce.7.cloned.1.call-done = f32[2048,64]{0,1:T(8,128)} async-done(((f32[2048,64]{0,1:T(8,128)}), f32[2048,64]{0,1:T(8,128)}) %all-reduce.7.cloned.1.call-update) | async-done | bytes 524304 | tf_op jit(solution)/shard_map/psum | solution.py:37
  296.5 1.8 fusion.17
  298.3 60.1 %psum.52 = f32[64,64]{0,1:T(8,128)S(1)} all-reduce(f32[64,64]{0,1:T(8,128)S(1)} %fusion.17), channel_id=1, replica_groups=mesh['series'=16,'tm'=16] {'tm'}, use_global_device_ids=true, to_apply=%region_5.0 | all-reduce | flops 4096 | bytes 32768 | tf_op jit(solution)/shard_map/psum | solution.py:38
  358.3 0.1 copy.9
  358.4 5.8 cholesky.70
  364.3 0.6 compare_reduce_fusion.1
  365.0 0.7 fusion.7
  365.6 4.9 custom-call.8
  370.5 1.7 fusion.2
  372.2 10.8 %convolution_bitcast_fusion = f32[2048,64]{0,1:T(8,128)} fusion(f32[64,2048]{1,0:T(8,128)S(1)} %fusion.2, bf16[2048,2048]{1,0:T(8,128)(2,1)} %param.5), kind=kOutput, calls=%fused_computation | convolution fusion | flops 3221225472 | bytes 9437184 | tf_op jit(solution)/shard_map/dot_general | solution.py:14
  383.0 0.0 all-reduce.9.cloned.1.call-update
  383.0 0.0 all-reduce.11.cloned.1.call-start
  383.1 0.8 multiply_bitcast_fusion.2
  383.9 0.8 multiply_bitcast_fusion.1
  384.8 102.0 %all-reduce.9.cloned.1.call-done = f32[2048,64]{0,1:T(8,128)} async-done(((f32[2048,64]{0,1:T(8,128)}), f32[2048,64]{0,1:T(8,128)}) %all-reduce.9.cloned.1.call-update) | async-done | bytes 524304 | tf_op jit(solution)/shard_map/psum | solution.py:40
  486.8 1.8 fusion.18
  488.6 45.5 %psum.54 = f32[64,64]{0,1:T(8,128)S(1)} all-reduce(f32[64,64]{0,1:T(8,128)S(1)} %fusion.18), channel_id=1, replica_groups=mesh['series'=16,'tm'=16] {'series'}, use_global_device_ids=true, to_apply=%region_7.10 | all-reduce | flops 4096 | bytes 32768 | tf_op jit(solution)/shard_map/psum | solution.py:41
  534.0 0.1 copy.11
  534.1 5.8 cholesky.81
  540.0 0.6 compare_reduce_fusion
  540.7 0.7 fusion.8
  541.3 4.9 custom-call.9
  546.2 1.7 fusion
  547.9 7.6 %fusion.19 = f32[64,2048]{1,0:T(8,128)} fusion(f32[64,2048]{1,0:T(8,128)S(1)} %fusion, bf16[2048,2048]{1,0:T(8,128)(2,1)} %param.5), kind=kOutput, calls=%fused_computation.38 | convolution fusion | flops 3221225472 | bytes 9437184 | tf_op jit(solution)/shard_map/dot_general | solution.py:18
  555.5 0.0 all-reduce.11.cloned.1.call-update
  555.5 0.8 multiply_bitcast_fusion
  556.4 109.7 %all-reduce.11.cloned.1.call-done = f32[64,2048]{1,0:T(8,128)} async-done(((f32[64,2048]{1,0:T(8,128)}), f32[64,2048]{1,0:T(8,128)}) %all-reduce.11.cloned.1.call-update) | async-done | bytes 524304 | tf_op jit(solution)/shard_map/psum | solution.py:43
  666.1 1.9 copy.19
  (6 shorter events, 0.1 us)
Async XLA Ops:
  7.2 1.0 copy-start
  7.2 109.8 %all-reduce.5.cloned.1.call-start = ((), (), s32[]{:S(2)}) async-start(), calls=%async_computation | async-start | bytes 1048576 | tf_op jit(solution)/shard_map/psum | solution.py:34
  19.0 277.4 %all-reduce.7.cloned.1.call-start = ((), (), s32[]{:S(2)}) async-start(), calls=%async_computation.1 | async-start | bytes 1048576 | tf_op jit(solution)/shard_map/psum | solution.py:37
  185.7 301.1 %all-reduce.9.cloned.1.call-start = ((), (), s32[]{:S(2)}) async-start(), calls=%async_computation.2 | async-start | bytes 1048576 | tf_op jit(solution)/shard_map/psum | solution.py:40
  383.0 283.1 %all-reduce.11.cloned.1.call-start = ((), (), s32[]{:S(2)}) async-start(), calls=%async_computation.3 | async-start | bytes 1048576 | tf_op jit(solution)/shard_map/psum | solution.py:43
Sparse Core Ops, SparseCore 0:
  19.2 97.7 all-reduce.4
  185.8 110.6 all-reduce.6
  383.2 103.6 all-reduce.8
  555.7 110.4 all-reduce.10
where the time goes:
time: 675 us
  waiting for transfers between devices  420 us (62%)
  blocking collectives  151 us (22%)
  matrix products  47.2 us (7%)
  other arithmetic  38.8 us (6%)
  between operations  13.9 us (2%)
    psum x1, waiting for transfers between devices, local(): back = lax.psum(left_apply(traffic, first_basis), 'series')  111 us
    psum x1, waiting for transfers between devices, local(): projection = lax.psum(left_apply(final_basis, traffic), 'series')  110 us
    psum x1, waiting for transfers between devices, local(): forward = lax.psum(right_apply(traffic, back_basis), 'tm')  102 us
    psum x1, waiting for transfers between devices, local(): sampled = lax.psum(right_apply(traffic, sketch), 'tm')  97.9 us
    psum x1, blocking collectives, local(): gram_two = lax.psum(gram_of(back), 'tm')  60.1 us
    psum x1, blocking collectives, local(): gram_three = lax.psum(gram_of(forward), 'series')  45.5 us
    psum x1, blocking collectives, local(): gram_one = lax.psum(gram_of(sampled), 'series')  45.5 us
    dot_general x2, matrix products, right_apply(): jnp.dot(tile, panel, precision=lax.Precision.HIGHEST, preferred_element_t...  21.6 us
  transfers between devices with their start and end apart: 4, of which 4 were waited for; matrix products, arithmetic and copies ran while one was open for 0% of the time, Pallas kernels for 0%

commit v1 on v0

v1 whole, which is shorter than its diff:
```python
import functools

import jax
import jax.numpy as jnp
from jax import lax
from jax.experimental import pallas as pl
from jax.experimental.pallas import tpu as pltpu
from jax.sharding import PartitionSpec as P

F32, BF16 = jnp.float32, jnp.bfloat16
HIGHEST = lax.Precision.HIGHEST
MESH = pl.DeviceIdType.MESH
LANES = 128
PAIR = 2 * LANES
NN = (((1,), (0,)), ((), ()))
NT = (((1,), (1,)), ((), ()))
CUTS = (24, 48)


def far_first(k, n):
    half = n // 2
    return (k + half + k // half + half * (k // (n - 1))) % n


def exact(x, y, dims=NN):
    return lax.dot_general(x, y, dims, precision=HIGHEST, preferred_element_type=F32)


def kernel(
    n_s, n_t, a_hbm, sketch, first_out, back_out, basis_out, proj_out,
    a, lhs, tm_part, tm_in, tm_full, z_part, sib_in, z_send, z_in, z_full, flats, back_flat, basis_flat, invs, work,
    g_out, g_tm, g_z, g_half, g_sib,
    a_sem, tm_rs_s, tm_rs_r, tm_ag_s, tm_ag_r, sib_s, sib_r, z_rs_s, z_rs_r, z_ag_s, z_ag_r, fw_s, fw_r,
    g_s, g_r, gs_s, gs_r,
):
    n_z, n_p = n_s // 2, n_t // 2
    k_all = sketch.shape[0]
    k_half = k_all // 2
    rows, cols = a.shape
    rows_total, cols_total = rows * n_s, cols * n_t
    s, t = lax.axis_index("series"), lax.axis_index("tm")
    z, core, p_me = s // 2, s % 2, t // 2
    halves = (pl.ds(0, k_half), pl.ds(k_half, k_half))

    def remote(src, dst, send, recv, to_s, to_t):
        return pltpu.make_async_remote_copy(
            src_ref=src, dst_ref=dst, send_sem=send, recv_sem=recv, device_id=(to_s, to_t), device_id_type=MESH
        )

    def to_sibling(src, dst, send, recv):
        return remote(src, dst, send, recv, 2 * z + 1 - core, t)

    def settle(ref, sem):
        pltpu.make_async_copy(ref, ref, sem).wait()

    def loop(n, body):
        def step(k, carry):
            body(k)
            return carry

        lax.fori_loop(0, n, step, 0)

    barrier = pltpu.get_barrier_semaphore()

    def greet_tm(k):
        pl.semaphore_signal(barrier, inc=1, device_id=(s, (t + 1 + k) % n_t), device_id_type=MESH)

    def greet_z(k):
        pl.semaphore_signal(barrier, inc=1, device_id=(2 * ((z + 1 + k) % n_z) + core, t), device_id_type=MESH)

    loop(n_t - 1, greet_tm)
    loop(n_z - 1, greet_z)
    pl.semaphore_signal(barrier, inc=1, device_id=(2 * z + 1 - core, t), device_id_type=MESH)

    def a_copy(k):
        p = (p_me + far_first(k, n_p)) % n_p
        block = pl.ds(pl.multiple_of(p * PAIR, PAIR), PAIR)
        return pltpu.make_async_copy(a_hbm.at[block, :], a.at[block, :], a_sem.at[k])

    loop(n_p, lambda k: a_copy(k).start())

    def split(x, h, lanes):
        for term in range(3):
            low = x.astype(BF16)
            lhs[pl.ds((3 * h + term) * k_half, k_half), lanes] = low
            x = x - low.astype(F32)

    def join(acc, h):
        b = 3 * h * k_half
        return acc[b : b + k_half] + (acc[b + k_half : b + 2 * k_half] + acc[b + 2 * k_half : b + 3 * k_half])

    for h in range(2):
        split(sketch[halves[h], :], h, slice(None))

    def tm_product(stage, ready):
        part, into = tm_part.at[stage], tm_in.at[stage]

        def send(k, h):
            p = (p_me + far_first(k, n_p)) % n_p
            for e in range(2):
                to = 2 * p + e

                @pl.when(to != t)
                def _():
                    remote(
                        part.at[to, halves[h], :], into.at[(t - to - 1 + n_t) % n_t, halves[h], :],
                        tm_rs_s.at[stage, h], tm_rs_r.at[stage, h], s, to,
                    ).start()

        def body(k):
            if ready is not None:
                ready(k)
            p = (p_me + far_first(k, n_p)) % n_p
            block = a[pl.ds(pl.multiple_of(p * PAIR, PAIR), PAIR), :]
            acc = lax.dot_general(lhs[...], block, NT, preferred_element_type=F32)
            for h in range(2):
                val = join(acc, h)
                for e in range(2):
                    part[2 * p + e, halves[h], :] = val[:, e * LANES : (e + 1) * LANES]
            send(k, 0)

        loop(n_p, body)
        loop(n_p, lambda k: send(k, 1))

    def tm_sum(stage, h):
        settle(tm_in.at[stage, :, halves[h], :], tm_rs_r.at[stage, h])
        total = tm_part[stage, t, halves[h], :]
        for i in range(n_t - 1):
            total = total + tm_in[stage, i, halves[h], :]
        return total

    def tm_gather(stage, h, chunk):
        tm_full[stage, t, halves[h], :] = chunk

        def send(k):
            mine = tm_full.at[stage, t, halves[h], :]
            to = (t + 1 + (k + n_t // 2 - 1) % (n_t - 1)) % n_t
            remote(mine, mine, tm_ag_s.at[stage, h], tm_ag_r.at[stage, h], s, to).start()

        loop(n_t - 1, send)

    def tm_take(stage, h, flat):
        settle(tm_full.at[stage, pl.ds(0, n_t - 1), halves[h], :], tm_ag_r.at[stage, h])
        for c in range(n_t):
            lanes = pl.ds(c * LANES, LANES)
            x = tm_full[stage, c, halves[h], :]
            flat[halves[h], lanes] = x
            split(x, h, lanes)

    def z_product(stage):
        part = z_part.at[stage]

        def pair(k):
            return (z + far_first(k, n_z)) % n_z

        def sibling(p):
            return to_sibling(part.at[1 - core, p], sib_in.at[stage, p], sib_s.at[stage, p], sib_r.at[stage, p])

        def send(k, h):
            p = pair(k)
            remote(
                z_send.at[stage, p, halves[h], :], z_in.at[stage, (z - p - 1 + n_z) % n_z, halves[h], :],
                z_rs_s.at[stage, h], z_rs_r.at[stage, h], 2 * p + core, t,
            ).start()

        def both(k):
            p = pair(k)
            sibling(p).wait_recv()
            z_send[stage, p] = part[core, p] + sib_in[stage, p]

        def body(k):
            p = pair(k)
            block = a[:, pl.ds(pl.multiple_of(p * PAIR, PAIR), PAIR)]
            acc = lax.dot_general(lhs[...], block, NN, preferred_element_type=F32)
            for h in range(2):
                val = join(acc, h)
                for e in range(2):
                    part[e, p, halves[h], :] = val[:, e * LANES : (e + 1) * LANES]
            sibling(p).start()

            @pl.when(k > 0)
            def _():
                both(k - 1)
                send(k - 1, 0)

        loop(n_z, body)
        loop(n_z - 1, lambda k: send(k, 1))
        both(n_z - 1)

    def z_sum(stage, h):
        settle(z_in.at[stage, :, halves[h], :], z_rs_r.at[stage, h])
        total = z_send[stage, z, halves[h], :]
        for i in range(n_z - 1):
            total = total + z_in[stage, i, halves[h], :]
        return total

    def z_gather(stage, h, chunk):
        z_full[stage, core, z, halves[h], :] = chunk

        def send(k):
            mine = z_full.at[stage, core, z, halves[h], :]
            to = (z + far_first(k, n_z)) % n_z
            remote(mine, mine, z_ag_s.at[stage, h], z_ag_r.at[stage, h], 2 * to + core, t).start()

        loop(n_z - 1, send)

    def z_forward(stage, h):
        settle(z_full.at[stage, core, pl.ds(0, n_z - 1), halves[h], :], z_ag_r.at[stage, h])
        mine = z_full.at[stage, core, :, halves[h], :]
        to_sibling(mine, mine, fw_s.at[stage, h], fw_r.at[stage, h]).start()

    def z_take(stage, h, flat, again=True):
        settle(z_full.at[stage, core, :, halves[h], :], fw_r.at[stage, h])
        for c in range(n_s):
            lanes = pl.ds(c * LANES, LANES)
            x = z_full[stage, c % 2, c // 2, halves[h], :]
            flat[halves[h], lanes] = x
            if again:
                split(x, h, lanes)

    def pack(flat, out):
        gram = exact(flat[...], flat[...], NT)
        out[:, :k_all] = gram[:k_half]
        out[:, k_all:] = gram[k_half:]

    def unpack(packed):
        lane = lax.broadcasted_iota(jnp.int32, (k_all, 2 * k_all), 1)
        row = lax.broadcasted_iota(jnp.int32, (k_all, 2 * k_all), 0)
        work[...] = jnp.where(lane == row + k_all, 1.0, 0.0).astype(F32)
        work[:k_half, :k_all] = packed[:, :k_all]
        work[k_half:, :k_all] = packed[:, k_all:]

    def gram_z_send(i, flat):
        pack(flat, g_out.at[i])
        slot = g_z.at[i // 2, z]
        slot[...] = g_out[i]

        def send(k):
            to = (z + far_first(k, n_z)) % n_z
            remote(g_out.at[i], slot, g_s.at[i], g_r.at[i], 2 * to + core, t).start()

        loop(n_z - 1, send)

    def gram_z_middle(i):
        b = i // 2
        settle(g_z.at[b, pl.ds(0, n_z - 1)], g_r.at[i])
        total = g_z[b, 0]
        for k in range(1, n_z):
            total = total + g_z[b, k]
        g_half[b] = total
        to_sibling(g_half.at[b], g_sib.at[b], gs_s.at[b], gs_r.at[b]).start()

    def gram_z_end(i):
        b = i // 2
        settle(g_sib.at[b], gs_r.at[b])
        unpack(g_half[b] + g_sib[b])

    def gram_tm_send(i, flat):
        pack(flat, g_out.at[i])
        slot = g_tm.at[t]
        slot[...] = g_out[i]

        def send(k):
            to = (t + 1 + (k + n_t // 2 - 1) % (n_t - 1)) % n_t
            remote(g_out.at[i], slot, g_s.at[i], g_r.at[i], s, to).start()

        loop(n_t - 1, send)

    def gram_tm_end(i):
        settle(g_tm.at[pl.ds(0, n_t - 1)], g_r.at[i])
        total = g_tm[0]
        for k in range(1, n_t):
            total = total + g_tm[k]
        unpack(total)

    def eliminate(start, stop):
        x = work[...]
        row = lax.broadcasted_iota(jnp.int32, (k_all, 1), 0)
        for j in range(start, stop):
            factor = jnp.where(row > j, x[:, j : j + 1] * (1.0 / x[j : j + 1, j : j + 1]), 0.0)
            x = x - factor * x[j : j + 1, :]
        work[...] = x

    def inverse(i):
        x = work[...]
        lane = lax.broadcasted_iota(jnp.int32, (k_all, 2 * k_all), 1)
        row = lax.broadcasted_iota(jnp.int32, (k_all, 2 * k_all), 0)
        diag = jnp.sum(jnp.where(lane == row, x, 0.0), axis=1, keepdims=True)
        invs[i] = (x * lax.rsqrt(diag))[:, k_all:]

    def apply_a(i, low):
        return exact(invs[i, :k_half, :k_half], low)

    def apply_b(i, low, high):
        return exact(invs[i, k_half:, :k_half], low) + exact(invs[i, k_half:, k_half:], high)

    cut_1, cut_2 = CUTS

    def ready(k):
        a_copy(k).wait()

        @pl.when(k == 0)
        def _():
            pl.semaphore_wait(barrier, n_t - 1 + n_z - 1 + 1)

    tm_product(0, ready)
    for h in range(2):
        tm_gather(0, h, tm_sum(0, h))
    for h in range(2):
        tm_take(0, h, flats.at[0])

    gram_z_send(0, flats.at[0])
    z_product(0)
    z_gather(0, 0, z_sum(0, 0))
    gram_z_middle(0)
    z_gather(0, 1, z_sum(0, 1))
    gram_z_end(0)
    eliminate(0, cut_1)
    z_forward(0, 0)
    eliminate(cut_1, cut_2)
    z_forward(0, 1)
    eliminate(cut_2, k_all)
    inverse(0)
    for h in range(2):
        z_take(0, h, flats.at[1])

    back_flat[...] = exact(invs[0], flats[1])
    gram_tm_send(1, back_flat)
    tm_product(1, None)
    first_out[...] = (rows_total**0.5) * exact(invs[0], flats[0])
    low = tm_sum(1, 0)
    tm_gather(1, 0, apply_a(0, low))
    high = tm_sum(1, 1)
    tm_gather(1, 1, apply_b(0, low, high))
    gram_tm_end(1)
    eliminate(0, cut_1)
    tm_take(1, 0, flats.at[2])
    eliminate(cut_1, k_all)
    inverse(1)
    tm_take(1, 1, flats.at[2])

    basis_flat[...] = exact(invs[1], flats[2])
    gram_z_send(2, basis_flat)
    z_product(1)
    back_out[...] = (cols_total**0.5) * exact(invs[1], back_flat[...])
    low = z_sum(1, 0)
    z_gather(1, 0, apply_a(1, low))
    gram_z_middle(2)
    high = z_sum(1, 1)
    z_gather(1, 1, apply_b(1, low, high))
    gram_z_end(2)
    eliminate(0, cut_1)
    z_forward(1, 0)
    eliminate(cut_1, cut_2)
    z_forward(1, 1)
    eliminate(cut_2, k_all)
    inverse(2)
    basis_out[...] = (rows_total**0.5) * exact(invs[2], basis_flat[...])
    for h in range(2):
        z_take(1, h, flats.at[3], again=False)
    proj_out[...] = exact(invs[2], flats[3])

    for stage in range(2):
        for h in range(2):
            settle(tm_in.at[stage, :, halves[h], :], tm_rs_s.at[stage, h])
            settle(tm_full.at[stage, pl.ds(0, n_t - 1), halves[h], :], tm_ag_s.at[stage, h])
            settle(z_in.at[stage, :, halves[h], :], z_rs_s.at[stage, h])
            settle(z_full.at[stage, core, pl.ds(0, n_z - 1), halves[h], :], z_ag_s.at[stage, h])
            settle(z_full.at[stage, core, :, halves[h], :], fw_s.at[stage, h])
        for p in range(n_z):
            settle(sib_in.at[stage, p], sib_s.at[stage, p])
        settle(g_z.at[stage, pl.ds(0, n_z - 1)], g_s.at[2 * stage])
        settle(g_sib.at[stage], gs_s.at[stage])
    settle(g_tm.at[pl.ds(0, n_t - 1)], g_s.at[1])


def solution(mesh):
    n_s, n_t = mesh.shape["series"], mesh.shape["tm"]
    n_z = n_s // 2

    def local(traffic, sketch):
        rows, cols = traffic.shape
        k = sketch.shape[1]
        vmem = pl.BlockSpec(memory_space=pltpu.VMEM)
        sem = pltpu.SemaphoreType.DMA
        chunk = (k, LANES)
        gram = (k // 2, 2 * k)
        outs = pl.pallas_call(
            functools.partial(kernel, n_s, n_t),
            out_shape=(
                jax.ShapeDtypeStruct((k, rows), F32),
                jax.ShapeDtypeStruct((k, cols), F32),
                jax.ShapeDtypeStruct((k, rows), F32),
                jax.ShapeDtypeStruct((k, cols), F32),
            ),
            in_specs=[pl.BlockSpec(memory_space=pl.ANY), vmem],
            out_specs=(vmem,) * 4,
            scratch_shapes=[
                pltpu.VMEM((rows, cols), BF16),
                pltpu.VMEM((3 * k, cols), BF16),
                pltpu.VMEM((2, n_t, *chunk), F32),
                pltpu.VMEM((2, n_t - 1, *chunk), F32),
                pltpu.VMEM((2, n_t, *chunk), F32),
                pltpu.VMEM((2, 2, n_z, *chunk), F32),
                pltpu.VMEM((2, n_z, *chunk), F32),
                pltpu.VMEM((2, n_z, *chunk), F32),
                pltpu.VMEM((2, n_z - 1, *chunk), F32),
                pltpu.VMEM((2, 2, n_z, *chunk), F32),
                pltpu.VMEM((4, k, cols), F32),
                pltpu.VMEM((k, cols), F32),
                pltpu.VMEM((k, rows), F32),
                pltpu.VMEM((3, k, k), F32),
                pltpu.VMEM((k, 2 * k), F32),
                pltpu.VMEM((3, *gram), F32),
                pltpu.VMEM((n_t, *gram), F32),
                pltpu.VMEM((2, n_z, *gram), F32),
                pltpu.VMEM((2, *gram), F32),
                pltpu.VMEM((2, *gram), F32),
                sem((n_t // 2,)),
                sem((2, 2)), sem((2, 2)), sem((2, 2)), sem((2, 2)),
                sem((2, n_z)), sem((2, n_z)),
                sem((2, 2)), sem((2, 2)), sem((2, 2)), sem((2, 2)), sem((2, 2)), sem((2, 2)),
                sem((3,)), sem((3,)), sem((2,)), sem((2,)),
            ],
            compiler_params=pltpu.CompilerParams(
                collective_id=0, has_side_effects=True, vmem_limit_bytes=48 * 2**20
            ),
            name="range_finder",
        )(traffic, sketch.T)
        return outs[0].T, outs[1].T, outs[2].T, outs[3]

    in_specs = (P("series", "tm"), P("tm", None))
    out_specs = (P("series", None), P("tm", None), P("series", None), P(None, "tm"))
    return jax.shard_map(local, mesh=mesh, in_specs=in_specs, out_specs=out_specs, check_vma=False)
```

time: 675 us -> 99.6 us (0.15)
  waiting for transfers between devices: 420 us -> 0 us
  blocking collectives: 151 us -> 0 us
  Pallas kernels: 0 us -> 94.6 us
  matrix products: 47.2 us -> 0 us
  other arithmetic: 38.8 us -> 0 us
  between operations: 13.9 us -> 0.65 us
    psum x4 -> x0, waiting for transfers between devices: 420 us -> none  [the longest x1 111 us: local(): back = lax.psum(left_apply(traffic, first_basis), 'series')]
    psum x3 -> x0, blocking collectives: 151 us -> none  [the longest x1 60.1 us: local(): gram_two = lax.psum(gram_of(back), 'tm')]
    pallas_call x0 -> x1, Pallas kernels: none -> 94.6 us  [local(): pl.pallas_call(functools.partial(kernel, n_s, n_t), out_shape=(jax.ShapeD...]
    dot_general x7 -> x0, matrix products: 42.1 us -> none  [the longest x2 21.6 us: right_apply(): jnp.dot(tile, panel, precision=lax.Precision.HIGHEST, preferred_element_t...]
    another operation x15 -> x0, other arithmetic: 36.2 us -> none  [the longest x6 16.6 us: solve_right(): return jax.scipy.linalg.solve_triangular(lower, tall.T, lower=True).T]
  transfers between devices with their start and end apart: 4 -> 0, of which waited for: 4 -> 0; matrix products, arithmetic and copies ran while one was open for 0% -> 0% of each run, Pallas kernels for 0% -> 0%
where the time goes in v1:
time: 99.6 us; the launch traced here: 99.4 us
  Pallas kernels  94.6 us (95%)
  local copies, waits for them, and re-layouts  4.21 us (4%)
    pallas_call x1, Pallas kernels, local(): pl.pallas_call(functools.partial(kernel, n_s, n_t), out_shape=(jax.ShapeD...  94.6 us
    unnamed x6, local copies, waits for them, and re-layouts  4.21 us

profile of v1, /device:TPU:1, one launch (start us, length us, event | category | flops | bytes accessed | tf_op | source)
XLA Modules:
  0.0 99.4 jit_solution(222811088036885018)
XLA Ops:
  0.6 0.0 copy-start
  0.6 1.0 %copy-done = f32[2048,64]{0,1:T(8,128)S(1)} copy-done((f32[2048,64]{0,1:T(8,128)S(1)}, f32[2048,64]{0,1:T(8,128)}, u32[]{:S(2)}) %copy-start) | copy-done | bytes 524312
  1.7 94.6 %range_finder.1 = (f32[64,2048]{1,0:T(8,128)S(1)}, f32[64,2048]{1,0:T(8,128)S(1)}, f32[64,2048]{1,0:T(8,128)S(1)}, f32[64,2048]{1,0:T(8,128)S(1)}) custom-call(bf16[2048,2048]{1,0:T(8,128)(2,1)} %a_hbm.1, f32[64,2048]{1,0:T(8,128)S(1)} %bitcast.4), custom_call_target="tpu_custom_call" | custom-call | tf_op jit(solution)/shard_map/range_finder/pallas_call | solution.py:388
  96.3 0.8 copy.10
  97.0 0.8 copy.11
  97.8 0.8 copy.12
  98.6 0.8 copy.13
Async XLA Ops:
  0.6 1.0 %copy-start = (f32[2048,64]{0,1:T(8,128)S(1)}, f32[2048,64]{0,1:T(8,128)}, u32[]{:S(2)}) copy-start(f32[2048,64]{0,1:T(8,128)} %param.3) | copy-start | bytes 1572868

commit v2 on v0

v2 whole, which is shorter than its diff:
```python
import functools
import math

import jax
import jax.numpy as jnp
from jax import lax
from jax.experimental import pallas as pl
from jax.experimental.pallas import tpu as pltpu
from jax.sharding import PartitionSpec as P

F32, BF16 = jnp.float32, jnp.bfloat16
HIGHEST = lax.Precision.HIGHEST
MESH = pl.DeviceIdType.MESH
LANES = 128
PANEL = 8
NN = (((1,), (0,)), ((), ()))
NT = (((1,), (1,)), ((), ()))


def far_first(n):
    return sorted(range(n), key=lambda d: (-min(d, n - d), d))


def exact(x, y, dims=NN):
    return lax.dot_general(x, y, dims, precision=HIGHEST, preferred_element_type=F32)


def kernel(
    n_s, n_t, a_hbm, sketch_hbm, first_out, back_out, basis_out, proj_out, inv_out,
    a, sketch, lhs, tm_part, tm_in, tm_full, z_part, sib_in, z_send, z_in, z_full, flats, back_flat, basis_flat, tm_low, z_low, invs, work,
    g_out, g_tm, g_z, g_half, g_sib,
    a_sem, s_sem, tm_rs_s, tm_rs_r, tm_ag_s, tm_ag_r, sib_s, sib_r, z_rs_s, z_rs_r, z_ag_s, z_ag_r, fw_s, fw_r,
    g_s, g_r, gs_s, gs_r,
):
    n_z, n_g = n_s // 2, n_s // 4
    n_x = math.isqrt(n_t)
    n_y = n_t // n_x
    k_all = sketch.shape[0]
    k_half = k_all // 2
    rows, cols = a.shape
    rows_total, cols_total = rows * n_s, cols * n_t
    s, t = lax.axis_index("series"), lax.axis_index("tm")
    z, core, y, x = s // 2, s % 2, t // n_x, t % n_x
    other = 2 * z + 1 - core
    halves = (pl.ds(0, k_half), pl.ds(k_half, k_half))

    tm_y = {d: (y + d) % n_y for d in range(n_y)}
    tm_x = {d: (x + d) % n_x for d in range(n_x)}
    tm_to = {(dy, dx): tm_y[dy] * n_x + tm_x[dx] for dy in range(n_y) for dx in range(n_x)}
    z_to = {d: (z + d) % n_z for d in range(n_z)}
    z_group = {d: (z // 2 + d) % n_g for d in range(n_g)}
    tm_order = sorted((o for o in tm_to if o != (0, 0)), key=lambda o: -min(o[0], n_y - o[0]) - min(o[1], n_x - o[1]))
    z_order = [d for d in far_first(n_z) if d]

    def remote(src, dst, send, recv, to_s, to_t):
        return pltpu.make_async_remote_copy(
            src_ref=src, dst_ref=dst, send_sem=send, recv_sem=recv, device_id=(to_s, to_t), device_id_type=MESH
        )

    def settle(ref, sem):
        pltpu.make_async_copy(ref, ref, sem).wait()

    barrier = pltpu.get_barrier_semaphore()
    greeted = [(s, tm_to[o]) for o in tm_order] + [(2 * z_to[d] + core, t) for d in z_order] + [(other, t)]
    for device in greeted:
        pl.semaphore_signal(barrier, inc=1, device_id=device, device_id_type=MESH)

    block_rows = n_x * LANES

    def tm_block(dy):
        return pl.ds(pl.multiple_of(tm_y[dy] * block_rows, block_rows), block_rows)

    sketch_copy = pltpu.make_async_copy(sketch_hbm, sketch, s_sem)
    sketch_copy.start()
    a_copies = {dy: pltpu.make_async_copy(a_hbm.at[tm_block(dy), :], a.at[tm_block(dy), :], a_sem.at[dy]) for dy in range(n_y)}
    for dy in far_first(n_y):
        a_copies[dy].start()

    def split(v, h, lanes):
        for term in range(3):
            low = v.astype(BF16)
            lhs[pl.ds((3 * h + term) * k_half, k_half), lanes] = low
            v = v - low.astype(F32)

    def terms(h):
        return lhs[pl.ds(3 * h * k_half, 3 * k_half), :]

    def join(acc):
        return acc[:k_half] + (acc[k_half : 2 * k_half] + acc[2 * k_half :])

    def tm_product(stage, h, between=None, ready=None):
        for i, dy in enumerate(far_first(n_y)):
            if ready is not None:
                ready(dy)
            acc = lax.dot_general(terms(h), a[tm_block(dy), :], NT, preferred_element_type=F32)
            val = join(acc)
            for e in range(n_x):
                tm_part[stage, tm_y[dy] * n_x + e, halves[h], :] = val[:, e * LANES : (e + 1) * LANES]
            for dx in far_first(n_x):
                if (dy, dx) != (0, 0):
                    to = tm_to[dy, dx]
                    remote(
                        tm_part.at[stage, to, halves[h], :], tm_in.at[stage, t, halves[h], :],
                        tm_rs_s.at[stage, h], tm_rs_r.at[stage, h], s, to,
                    ).start()
            if between and i == min(between[0], n_y - 1):
                between[1]()

    def tm_sum(stage, h):
        settle(tm_in.at[stage, pl.ds(0, n_t - 1), halves[h], :], tm_rs_r.at[stage, h])
        tm_in[stage, t, halves[h], :] = tm_part[stage, t, halves[h], :]
        total = tm_in[stage, 0, halves[h], :]
        for i in range(1, n_t):
            total = total + tm_in[stage, i, halves[h], :]
        return total

    def tm_gather(stage, h, chunk):
        tm_full[stage, t, halves[h], :] = chunk
        mine = tm_full.at[stage, t, halves[h], :]
        for o in tm_order:
            remote(mine, mine, tm_ag_s.at[stage, h], tm_ag_r.at[stage, h], s, tm_to[o]).start()

    def tm_take(stage, h, flat):
        settle(tm_full.at[stage, pl.ds(0, n_t - 1), halves[h], :], tm_ag_r.at[stage, h])
        for c in range(n_t):
            lanes = pl.ds(c * LANES, LANES)
            v = tm_full[stage, c, halves[h], :]
            flat[halves[h], lanes] = v
            split(v, h, lanes)

    def z_pair(dg):
        return pl.ds(2 * z_group[dg], 2)

    def sibling(stage, h, dg):
        return remote(
            z_part.at[stage, 1 - core, z_pair(dg), halves[h], :], sib_in.at[stage, z_pair(dg), halves[h], :],
            sib_s.at[stage, h, dg], sib_r.at[stage, h, dg], other, t,
        )

    def z_both(stage, h, dg):
        sibling(stage, h, dg).wait_recv()
        pair = z_pair(dg)
        z_send[stage, pair, halves[h], :] = z_part[stage, core, pair, halves[h], :] + sib_in[stage, pair, halves[h], :]
        tos = [2 * z_group[dg] + e for e in range(2)] if dg else [4 * (z // 2) + 1 - z]
        for to in tos:
            remote(
                z_send.at[stage, to, halves[h], :], z_in.at[stage, z, halves[h], :],
                z_rs_s.at[stage, h], z_rs_r.at[stage, h], 2 * to + core, t,
            ).start()

    def z_product(stage, h, between=None):
        before = None
        for i, dg in enumerate(far_first(n_g)):
            block = pl.ds(pl.multiple_of(z_group[dg] * 4 * LANES, 4 * LANES), 4 * LANES)
            acc = lax.dot_general(terms(h), a[:, block], NN, preferred_element_type=F32)
            val = join(acc)
            for e in range(4):
                z_part[stage, e % 2, 2 * z_group[dg] + e // 2, halves[h], :] = val[:, e * LANES : (e + 1) * LANES]
            sibling(stage, h, dg).start()
            if before is not None:
                z_both(stage, h, before)
            before = dg
            if between and i == min(between[0], n_g - 1):
                between[1]()

    def z_sum(stage, h):
        settle(z_in.at[stage, pl.ds(0, n_z - 1), halves[h], :], z_rs_r.at[stage, h])
        z_in[stage, z, halves[h], :] = z_send[stage, z, halves[h], :]
        total = z_in[stage, 0, halves[h], :]
        for i in range(1, n_z):
            total = total + z_in[stage, i, halves[h], :]
        return total

    def z_gather(stage, h, chunk):
        z_full[stage, core, z, halves[h], :] = chunk
        mine = z_full.at[stage, core, z, halves[h], :]
        for d in z_order:
            remote(mine, mine, z_ag_s.at[stage, h], z_ag_r.at[stage, h], 2 * z_to[d] + core, t).start()

    def z_forward(stage, h):
        settle(z_full.at[stage, core, pl.ds(0, n_z - 1), halves[h], :], z_ag_r.at[stage, h])
        mine = z_full.at[stage, core, :, halves[h], :]
        remote(mine, mine, fw_s.at[stage, h], fw_r.at[stage, h], other, t).start()

    def z_take(stage, h, flat, again=True):
        settle(z_full.at[stage, core, :, halves[h], :], fw_r.at[stage, h])
        for c in range(n_s):
            lanes = pl.ds(c * LANES, LANES)
            v = z_full[stage, c % 2, c // 2, halves[h], :]
            flat[halves[h], lanes] = v
            if again:
                split(v, h, lanes)

    def pack(flat, out):
        gram = exact(flat[...], flat[...], NT)
        out[:, :k_all] = gram[:k_half]
        out[:, k_all:] = gram[k_half:]

    def gram_z_send(i, flat):
        pack(flat, g_out.at[i])
        slot = g_z.at[i // 2, z]
        slot[...] = g_out[i]
        for d in z_order:
            remote(g_out.at[i], slot, g_s.at[i], g_r.at[i], 2 * z_to[d] + core, t).start()

    def gram_z_middle(i):
        b = i // 2
        settle(g_z.at[b, pl.ds(0, n_z - 1)], g_r.at[i])
        total = g_z[b, 0]
        for k in range(1, n_z):
            total = total + g_z[b, k]
        g_half[b] = total
        remote(g_half.at[b], g_sib.at[b], gs_s.at[b], gs_r.at[b], other, t).start()

    def gram_z_end(i):
        b = i // 2
        settle(g_sib.at[b], gs_r.at[b])
        return g_half[b] + g_sib[b]

    def gram_tm_send(i, flat):
        pack(flat, g_out.at[i])
        slot = g_tm.at[t]
        slot[...] = g_out[i]
        for o in tm_order:
            remote(g_out.at[i], slot, g_s.at[i], g_r.at[i], s, tm_to[o]).start()

    def gram_tm_end(i):
        settle(g_tm.at[pl.ds(0, n_t - 1)], g_r.at[i])
        total = g_tm[0]
        for k in range(1, n_t):
            total = total + g_tm[k]
        return total

    def invert(i, packed):
        lane = lax.broadcasted_iota(jnp.int32, (k_all, 2 * k_all), 1)
        row = lax.broadcasted_iota(jnp.int32, (k_all, 2 * k_all), 0)
        work[...] = jnp.where(lane == row + k_all, 1.0, 0.0).astype(F32)
        work[:k_half, :k_all] = packed[:, :k_all]
        work[k_half:, :k_all] = packed[:, k_all:]
        v = work[...]
        for j in range(0, k_all, PANEL):
            col = [jnp.broadcast_to(v[:, j + m : j + m + 1], v.shape) for m in range(PANEL)]
            line = [v[j + m : j + m + 1, :] for m in range(PANEL)]
            for m in range(PANEL):
                factor = jnp.where(row > j + m, col[m] * (1.0 / col[m][j + m : j + m + 1, :]), 0.0)
                for n in range(m + 1, PANEL):
                    line[n] = line[n] - factor[j + n : j + n + 1, :] * line[m]
                    col[n] = col[n] - factor * col[n][j + m : j + m + 1, :]
                v = v - factor * line[m]
        diag = jnp.sum(jnp.where(lane == row, v, 0.0), axis=1, keepdims=True)
        invs[i] = (v * lax.rsqrt(diag))[:, k_all:]

    def apply_a(i, low):
        return exact(invs[i, :k_half, :k_half], low)

    def apply_b(i, low, high):
        return exact(invs[i, k_half:, :k_half], low) + exact(invs[i, k_half:, k_half:], high)

    sketch_copy.wait()
    for h in range(2):
        split(sketch[halves[h], :], h, slice(None))

    def ready(dy):
        a_copies[dy].wait()
        if dy == far_first(n_y)[0]:
            pl.semaphore_wait(barrier, len(greeted))

    tm_product(0, 0, ready=ready)
    tm_product(0, 1)
    tm_gather(0, 0, tm_sum(0, 0))
    tm_gather(0, 1, tm_sum(0, 1))
    tm_take(0, 0, flats.at[0])

    z_product(0, 0)
    tm_take(0, 1, flats.at[0])
    z_both(0, 0, 0)
    z_product(0, 1, (2, lambda: z_gather(0, 0, z_sum(0, 0))))
    gram_z_send(0, flats.at[0])
    z_both(0, 1, 0)
    z_gather(0, 1, z_sum(0, 1))
    z_forward(0, 0)
    gram_z_middle(0)
    z_take(0, 0, flats.at[1])

    tm_product(1, 0)
    z_forward(0, 1)
    invert(0, gram_z_end(0))
    z_take(0, 1, flats.at[1])

    def tm_first_half():
        tm_low[...] = tm_sum(1, 0)
        tm_gather(1, 0, apply_a(0, tm_low[...]))

    tm_product(1, 1, (0, tm_first_half))
    back_flat[...] = exact(invs[0], flats[1])
    gram_tm_send(1, back_flat)
    first_out[...] = (rows_total**0.5) * exact(invs[0], flats[0])
    tm_gather(1, 1, apply_b(0, tm_low[...], tm_sum(1, 1)))
    tm_take(1, 0, flats.at[2])

    z_product(1, 0)
    z_both(1, 0, 0)
    invert(1, gram_tm_end(1))
    tm_take(1, 1, flats.at[2])

    def z_first_half():
        z_low[...] = z_sum(1, 0)
        z_gather(1, 0, apply_a(1, z_low[...]))

    z_product(1, 1, (1, z_first_half))
    basis_flat[...] = exact(invs[1], flats[2])
    gram_z_send(2, basis_flat)
    z_both(1, 1, 0)
    back_out[...] = (cols_total**0.5) * exact(invs[1], back_flat[...])
    z_gather(1, 1, apply_b(1, z_low[...], z_sum(1, 1)))
    z_forward(1, 0)
    gram_z_middle(2)
    invert(2, gram_z_end(2))
    inv_out[...] = invs[2]
    z_forward(1, 1)
    basis_out[...] = (rows_total**0.5) * exact(invs[2], basis_flat[...])
    for h in range(2):
        z_take(1, h, proj_out, again=False)

    for stage in range(2):
        for h in range(2):
            settle(tm_in.at[stage, pl.ds(0, n_t - 1), halves[h], :], tm_rs_s.at[stage, h])
            settle(z_in.at[stage, pl.ds(0, n_z - 1), halves[h], :], z_rs_s.at[stage, h])
            settle(tm_full.at[stage, pl.ds(0, n_t - 1), halves[h], :], tm_ag_s.at[stage, h])
            settle(z_full.at[stage, core, pl.ds(0, n_z - 1), halves[h], :], z_ag_s.at[stage, h])
            settle(z_full.at[stage, core, :, halves[h], :], fw_s.at[stage, h])
            for dg in range(n_g):
                settle(sib_in.at[stage, pl.ds(0, 2), halves[h], :], sib_s.at[stage, h, dg])
        settle(g_z.at[stage, pl.ds(0, n_z - 1)], g_s.at[2 * stage])
        settle(g_sib.at[stage], gs_s.at[stage])
    settle(g_tm.at[pl.ds(0, n_t - 1)], g_s.at[1])


def finish(first_in, back_in, basis_in, proj_in, inv, first_out, back_out, basis_out, proj_out, sems):
    pairs = ((first_in, first_out), (back_in, back_out), (basis_in, basis_out))
    copies = [pltpu.make_async_copy(src, dst, sems.at[i]) for i, (src, dst) in enumerate(pairs)]
    for copy in copies:
        copy.start()
    proj_out[...] = exact(inv[...], proj_in[...])
    for copy in copies:
        copy.wait()


def solution(mesh):
    n_s, n_t = mesh.shape["series"], mesh.shape["tm"]
    n_z, n_g = n_s // 2, n_s // 4

    def local(traffic, sketch):
        rows, cols = traffic.shape
        k = sketch.shape[1]
        vmem, hbm, anywhere = (pl.BlockSpec(memory_space=m) for m in (pltpu.VMEM, pltpu.HBM, pl.ANY))
        sem = pltpu.SemaphoreType.DMA
        chunk = (k, LANES)
        gram = (k // 2, 2 * k)
        by_rows, by_cols = jax.ShapeDtypeStruct((k, rows), F32), jax.ShapeDtypeStruct((k, cols), F32)
        outs = pl.pallas_call(
            functools.partial(kernel, n_s, n_t),
            out_shape=(by_rows, by_cols, by_rows, by_cols, jax.ShapeDtypeStruct((k, k), F32)),
            in_specs=[hbm, hbm],
            out_specs=(vmem,) * 5,
            scratch_shapes=[
                pltpu.VMEM((rows, cols), BF16),
                pltpu.VMEM((k, cols), F32),
                pltpu.VMEM((3 * k, cols), BF16),
                pltpu.VMEM((2, n_t, *chunk), F32),
                pltpu.VMEM((2, n_t, *chunk), F32),
                pltpu.VMEM((2, n_t, *chunk), F32),
                pltpu.VMEM((2, 2, n_z, *chunk), F32),
                pltpu.VMEM((2, n_z, *chunk), F32),
                pltpu.VMEM((2, n_z, *chunk), F32),
                pltpu.VMEM((2, n_z, *chunk), F32),
                pltpu.VMEM((2, 2, n_z, *chunk), F32),
                pltpu.VMEM((3, k, cols), F32),
                pltpu.VMEM((k, cols), F32),
                pltpu.VMEM((k, rows), F32),
                pltpu.VMEM((k // 2, LANES), F32),
                pltpu.VMEM((k // 2, LANES), F32),
                pltpu.VMEM((3, k, k), F32),
                pltpu.VMEM((k, 2 * k), F32),
                pltpu.VMEM((3, *gram), F32),
                pltpu.VMEM((n_t, *gram), F32),
                pltpu.VMEM((2, n_z, *gram), F32),
                pltpu.VMEM((2, *gram), F32),
                pltpu.VMEM((2, *gram), F32),
                sem((math.isqrt(n_t),)), sem,
                sem((2, 2)), sem((2, 2)), sem((2, 2)), sem((2, 2)),
                sem((2, 2, n_g)), sem((2, 2, n_g)),
                sem((2, 2)), sem((2, 2)), sem((2, 2)), sem((2, 2)), sem((2, 2)), sem((2, 2)),
                sem((3,)), sem((3,)), sem((2,)), sem((2,)),
            ],
            compiler_params=pltpu.CompilerParams(
                collective_id=0, has_side_effects=True, vmem_limit_bytes=48 * 2**20
            ),
            name="range_finder",
        )(traffic, sketch.T)
        first, back, basis, proj = pl.pallas_call(
            finish,
            out_shape=(by_rows, by_cols, by_rows, by_cols),
            in_specs=[anywhere] * 3 + [vmem] * 2,
            out_specs=(anywhere,) * 3 + (vmem,),
            scratch_shapes=[sem((3,))],
            compiler_params=pltpu.CompilerParams(vmem_limit_bytes=8 * 2**20),
            name="finish",
        )(*outs)
        return first.T, back.T, basis.T, proj

    in_specs = (P("series", "tm"), P("tm", None))
    out_specs = (P("series", None), P("tm", None), P("series", None), P(None, "tm"))
    return jax.shard_map(local, mesh=mesh, in_specs=in_specs, out_specs=out_specs, check_vma=False)
```

time: 675 us -> 87.1 us (0.13)
  waiting for transfers between devices: 420 us -> 0 us
  blocking collectives: 151 us -> 0 us
  Pallas kernels: 0 us -> 85.1 us
  matrix products: 47.2 us -> 0 us
  other arithmetic: 38.8 us -> 0 us
  between operations: 13.9 us -> 0.81 us
    psum x4 -> x0, waiting for transfers between devices: 420 us -> none  [the longest x1 111 us: local(): back = lax.psum(left_apply(traffic, first_basis), 'series')]
    psum x3 -> x0, blocking collectives: 151 us -> none  [the longest x1 60.1 us: local(): gram_two = lax.psum(gram_of(back), 'tm')]
    pallas_call x0 -> x2, Pallas kernels: none -> 85.1 us  [the longest x1 83.2 us: local(): pl.pallas_call(functools.partial(kernel, n_s, n_t), out_shape=(by_rows, b...]
    dot_general x7 -> x0, matrix products: 42.1 us -> none  [the longest x2 21.6 us: right_apply(): jnp.dot(tile, panel, precision=lax.Precision.HIGHEST, preferred_element_t...]
    another operation x15 -> x0, other arithmetic: 36.2 us -> none  [the longest x6 16.6 us: solve_right(): return jax.scipy.linalg.solve_triangular(lower, tall.T, lower=True).T]
  transfers between devices with their start and end apart: 4 -> 0, of which waited for: 4 -> 0; matrix products, arithmetic and copies ran while one was open for 0% -> 0% of each run, Pallas kernels for 0% -> 0%
where the time goes in v2:
time: 87.1 us; the launch traced here: 87 us
  Pallas kernels  85.1 us (98%)
  local copies, waits for them, and re-layouts  1.03 us (1%)
    pallas_call x1, Pallas kernels, local(): pl.pallas_call(functools.partial(kernel, n_s, n_t), out_shape=(by_rows, b...  83.2 us
    pallas_call x1, Pallas kernels, local(): pl.pallas_call(finish, out_shape=(by_rows, by_cols, by_rows, by_cols), in...  1.97 us

profile of v2, /device:TPU:1, one launch (start us, length us, event | category | flops | bytes accessed | tf_op | source)
XLA Modules:
  0.0 87.0 jit_solution(10009247356584702144)
XLA Ops:
  0.6 0.0 copy-start
  0.6 1.0 %copy-done = f32[2048,64]{0,1:T(8,128)S(1)} copy-done((f32[2048,64]{0,1:T(8,128)S(1)}, f32[2048,64]{0,1:T(8,128)}, u32[]{:S(2)}) %copy-start) | copy-done | bytes 524312
  1.7 83.2 %range_finder.1 = (f32[64,2048]{1,0:T(8,128)S(1)}, f32[64,2048]{1,0:T(8,128)S(1)}, f32[64,2048]{1,0:T(8,128)S(1)}, f32[64,2048]{1,0:T(8,128)S(1)}, f32[64,64]{1,0:T(8,128)S(1)}) custom-call(bf16[2048,2048]{1,0:T(8,128)(2,1)} %a_hbm.1, f32[64,2048]{1,0:T(8,128)S(1)} %bitcast.4), custom_call_target="tpu_custom_call" | custom-call | tf_op jit(solution)/shard_map/range_finder/pallas_call | solution.py:361
  84.8 2.0 %finish.1 = (f32[64,2048]{1,0:T(8,128)}, f32[64,2048]{1,0:T(8,128)}, f32[64,2048]{1,0:T(8,128)}, f32[64,2048]{1,0:T(8,128)}) custom-call(f32[64,2048]{1,0:T(8,128)S(1)} %get-tuple-element.13.first_in, f32[64,2048]{1,0:T(8,128)S(1)} %get-tuple-element.14.back_in, f32[64,2048]{1,0:T(8,128)S(1)} %get-tuple-element.15.basis_in, ...), custom_call_target="tpu_custom_call" | custom-call | tf_op jit(solution)/shard_map/finish/pallas_call | solution.py:401
Async XLA Ops:
  0.6 1.0 %copy-start = (f32[2048,64]{0,1:T(8,128)S(1)}, f32[2048,64]{0,1:T(8,128)}, u32[]{:S(2)}) copy-start(f32[2048,64]{0,1:T(8,128)} %param.3) | copy-start | bytes 1572868

commit v3 on v2

--- a/solution.py
+++ b/solution.py
@@ -26,17 +26,17 @@
 
 
 def kernel(
-    n_s, n_t, a_hbm, sketch_hbm, first_out, back_out, basis_out, proj_out, inv_out,
+    n_s, n_t, a_hbm, sketch_hbm, first_out, back_out, basis_out, proj_out,
     a, sketch, lhs, tm_part, tm_in, tm_full, z_part, sib_in, z_send, z_in, z_full, flats, back_flat, basis_flat, tm_low, z_low, invs, work,
-    g_out, g_tm, g_z, g_half, g_sib,
+    g_out, g_pair, g_tm, g_z, g_sum,
     a_sem, s_sem, tm_rs_s, tm_rs_r, tm_ag_s, tm_ag_r, sib_s, sib_r, z_rs_s, z_rs_r, z_ag_s, z_ag_r, fw_s, fw_r,
-    g_s, g_r, gs_s, gs_r,
+    gp_s, gp_r, g_s, g_r, gs_s, gs_r,
 ):
     n_z, n_g = n_s // 2, n_s // 4
     n_x = math.isqrt(n_t)
     n_y = n_t // n_x
     k_all = sketch.shape[0]
-    k_half = k_all // 2
+    k_half, k_quarter = k_all // 2, k_all // 4
     rows, cols = a.shape
     rows_total, cols_total = rows * n_s, cols * n_t
     s, t = lax.axis_index("series"), lax.axis_index("tm")
@@ -82,27 +82,28 @@
             lhs[pl.ds((3 * h + term) * k_half, k_half), lanes] = low
             v = v - low.astype(F32)
 
-    def terms(h):
-        return lhs[pl.ds(3 * h * k_half, 3 * k_half), :]
+    def terms(*hs):
+        return lhs[pl.ds(3 * hs[0] * k_half, 3 * len(hs) * k_half), :]
 
     def join(acc):
-        return acc[:k_half] + (acc[k_half : 2 * k_half] + acc[2 * k_half :])
-
-    def tm_product(stage, h, between=None, ready=None):
+        return acc[:k_half] + (acc[k_half : 2 * k_half] + acc[2 * k_half : 3 * k_half])
+
+    def tm_product(stage, hs, between=None, ready=None):
         for i, dy in enumerate(far_first(n_y)):
             if ready is not None:
                 ready(dy)
-            acc = lax.dot_general(terms(h), a[tm_block(dy), :], NT, preferred_element_type=F32)
-            val = join(acc)
-            for e in range(n_x):
-                tm_part[stage, tm_y[dy] * n_x + e, halves[h], :] = val[:, e * LANES : (e + 1) * LANES]
-            for dx in far_first(n_x):
-                if (dy, dx) != (0, 0):
-                    to = tm_to[dy, dx]
-                    remote(
-                        tm_part.at[stage, to, halves[h], :], tm_in.at[stage, t, halves[h], :],
-                        tm_rs_s.at[stage, h], tm_rs_r.at[stage, h], s, to,
-                    ).start()
+            acc = lax.dot_general(terms(*hs), a[tm_block(dy), :], NT, preferred_element_type=F32)
+            for h in hs:
+                val = join(acc[3 * (h - hs[0]) * k_half :])
+                for e in range(n_x):
+                    tm_part[stage, tm_y[dy] * n_x + e, halves[h], :] = val[:, e * LANES : (e + 1) * LANES]
+                for dx in far_first(n_x):
+                    if (dy, dx) != (0, 0):
+                        to = tm_to[dy, dx]
+                        remote(
+                            tm_part.at[stage, to, halves[h], :], tm_in.at[stage, t, halves[h], :],
+                            tm_rs_s.at[stage, h], tm_rs_r.at[stage, h], s, to,
+                        ).start()
             if between and i == min(between[0], n_y - 1):
                 between[1]()
 
@@ -193,15 +194,30 @@
 
     def pack(flat, out):
         gram = exact(flat[...], flat[...], NT)
-        out[:, :k_all] = gram[:k_half]
-        out[:, k_all:] = gram[k_half:]
+        for c in range(2):
+            out[c, :, :k_all] = gram[c * k_quarter : (c + 1) * k_quarter]
+            out[c, :, k_all:] = gram[k_half + c * k_quarter : k_half + (c + 1) * k_quarter]
+
+    def gram_swap(i, total):
+        g_sum[i, core] = total
+        mine = g_sum.at[i, core]
+        remote(mine, mine, gs_s.at[i], gs_r.at[i], other, t).start()
+
+    def gram_end(i):
+        settle(g_sum.at[i, core], gs_r.at[i])
+        return g_sum[i]
 
     def gram_z_send(i, flat):
         pack(flat, g_out.at[i])
-        slot = g_z.at[i // 2, z]
-        slot[...] = g_out[i]
+        remote(g_out.at[i, 1 - core], g_pair.at[i // 2], gp_s.at[i // 2], gp_r.at[i // 2], other, t).start()
+
+    def gram_z_pair(i):
+        b = i // 2
+        settle(g_pair.at[b], gp_r.at[b])
+        g_z[b, z] = g_out[i, core] + g_pair[b]
+        mine = g_z.at[b, z]
         for d in z_order:
-            remote(g_out.at[i], slot, g_s.at[i], g_r.at[i], 2 * z_to[d] + core, t).start()
+            remote(mine, mine, g_s.at[i], g_r.at[i], 2 * z_to[d] + core, t).start()
 
     def gram_z_middle(i):
         b = i // 2
@@ -209,34 +225,29 @@
         total = g_z[b, 0]
         for k in range(1, n_z):
             total = total + g_z[b, k]
-        g_half[b] = total
-        remote(g_half.at[b], g_sib.at[b], gs_s.at[b], gs_r.at[b], other, t).start()
-
-    def gram_z_end(i):
-        b = i // 2
-        settle(g_sib.at[b], gs_r.at[b])
-        return g_half[b] + g_sib[b]
+        gram_swap(i, total)
 
     def gram_tm_send(i, flat):
         pack(flat, g_out.at[i])
-        slot = g_tm.at[t]
-        slot[...] = g_out[i]
+        g_tm[t] = g_out[i, core]
+        mine = g_tm.at[t]
         for o in tm_order:
-            remote(g_out.at[i], slot, g_s.at[i], g_r.at[i], s, tm_to[o]).start()
-
-    def gram_tm_end(i):
+            remote(mine, mine, g_s.at[i], g_r.at[i], s, tm_to[o]).start()
+
+    def gram_tm_middle(i):
         settle(g_tm.at[pl.ds(0, n_t - 1)], g_r.at[i])
         total = g_tm[0]
         for k in range(1, n_t):
             total = total + g_tm[k]
-        return total
+        gram_swap(i, total)
 
     def invert(i, packed):
         lane = lax.broadcasted_iota(jnp.int32, (k_all, 2 * k_all), 1)
         row = lax.broadcasted_iota(jnp.int32, (k_all, 2 * k_all), 0)
         work[...] = jnp.where(lane == row + k_all, 1.0, 0.0).astype(F32)
-        work[:k_half, :k_all] = packed[:, :k_all]
-        work[k_half:, :k_all] = packed[:, k_all:]
+        for c in range(2):
+            work[pl.ds(c * k_quarter, k_quarter), :k_all] = packed[c, :, :k_all]
+            work[pl.ds(k_half + c * k_quarter, k_quarter), :k_all] = packed[c, :, k_all:]
         v = work[...]
         for j in range(0, k_all, PANEL):
             col = [jnp.broadcast_to(v[:, j + m : j + m + 1], v.shape) for m in range(PANEL)]
@@ -265,42 +276,44 @@
         if dy == far_first(n_y)[0]:
             pl.semaphore_wait(barrier, len(greeted))
 
-    tm_product(0, 0, ready=ready)
-    tm_product(0, 1)
-    tm_gather(0, 0, tm_sum(0, 0))
-    tm_gather(0, 1, tm_sum(0, 1))
+    tm_product(0, (0, 1), ready=ready)
+    for h in range(2):
+        tm_gather(0, h, tm_sum(0, h))
     tm_take(0, 0, flats.at[0])
 
     z_product(0, 0)
     tm_take(0, 1, flats.at[0])
     z_both(0, 0, 0)
     z_product(0, 1, (2, lambda: z_gather(0, 0, z_sum(0, 0))))
+    z_both(0, 1, 0)
     gram_z_send(0, flats.at[0])
-    z_both(0, 1, 0)
+    gram_z_pair(0)
     z_gather(0, 1, z_sum(0, 1))
     z_forward(0, 0)
-    gram_z_middle(0)
     z_take(0, 0, flats.at[1])
 
-    tm_product(1, 0)
-    z_forward(0, 1)
-    invert(0, gram_z_end(0))
+    def last_of_back():
+        gram_z_middle(0)
+        z_forward(0, 1)
+
+    tm_product(1, (0,), (2, last_of_back))
+    invert(0, gram_end(0))
     z_take(0, 1, flats.at[1])
 
     def tm_first_half():
         tm_low[...] = tm_sum(1, 0)
         tm_gather(1, 0, apply_a(0, tm_low[...]))
 
-    tm_product(1, 1, (0, tm_first_half))
+    tm_product(1, (1,), (0, tm_first_half))
     back_flat[...] = exact(invs[0], flats[1])
     gram_tm_send(1, back_flat)
     first_out[...] = (rows_total**0.5) * exact(invs[0], flats[0])
     tm_gather(1, 1, apply_b(0, tm_low[...], tm_sum(1, 1)))
     tm_take(1, 0, flats.at[2])
 
-    z_product(1, 0)
+    z_product(1, 0, (2, lambda: gram_tm_middle(1)))
     z_both(1, 0, 0)
-    invert(1, gram_tm_end(1))
+    invert(1, gram_end(1))
     tm_take(1, 1, flats.at[2])
 
     def z_first_half():
@@ -308,19 +321,21 @@
         z_gather(1, 0, apply_a(1, z_low[...]))
 
     z_product(1, 1, (1, z_first_half))
+    z_both(1, 1, 0)
     basis_flat[...] = exact(invs[1], flats[2])
     gram_z_send(2, basis_flat)
-    z_both(1, 1, 0)
+    gram_z_pair(2)
+    z_gather(1, 1, apply_b(1, z_low[...], z_sum(1, 1)))
     back_out[...] = (cols_total**0.5) * exact(invs[1], back_flat[...])
-    z_gather(1, 1, apply_b(1, z_low[...], z_sum(1, 1)))
     z_forward(1, 0)
     gram_z_middle(2)
-    invert(2, gram_z_end(2))
-    inv_out[...] = invs[2]
+    invert(2, gram_end(2))
     z_forward(1, 1)
     basis_out[...] = (rows_total**0.5) * exact(invs[2], basis_flat[...])
-    for h in range(2):
-        z_take(1, h, proj_out, again=False)
+    z_take(1, 0, flats.at[3], again=False)
+    proj_out[:k_half, :] = exact(invs[2, :k_half, :k_half], flats[3, :k_half, :])
+    z_take(1, 1, flats.at[3], again=False)
+    proj_out[k_half:, :] = exact(invs[2, k_half:, :], flats[3])
 
     for stage in range(2):
         for h in range(2):
@@ -332,16 +347,17 @@
             for dg in range(n_g):
                 settle(sib_in.at[stage, pl.ds(0, 2), halves[h], :], sib_s.at[stage, h, dg])
         settle(g_z.at[stage, pl.ds(0, n_z - 1)], g_s.at[2 * stage])
-        settle(g_sib.at[stage], gs_s.at[stage])
+        settle(g_pair.at[stage], gp_s.at[stage])
     settle(g_tm.at[pl.ds(0, n_t - 1)], g_s.at[1])
-
-
-def finish(first_in, back_in, basis_in, proj_in, inv, first_out, back_out, basis_out, proj_out, sems):
-    pairs = ((first_in, first_out), (back_in, back_out), (basis_in, basis_out))
-    copies = [pltpu.make_async_copy(src, dst, sems.at[i]) for i, (src, dst) in enumerate(pairs)]
+    for i in range(3):
+        settle(g_sum.at[i, core], gs_s.at[i])
+
+
+def finish(*refs):
+    sems = refs[-1]
+    copies = [pltpu.make_async_copy(refs[i], refs[4 + i], sems.at[i]) for i in range(4)]
     for copy in copies:
         copy.start()
-    proj_out[...] = exact(inv[...], proj_in[...])
     for copy in copies:
         copy.wait()
 
@@ -356,13 +372,13 @@
         vmem, hbm, anywhere = (pl.BlockSpec(memory_space=m) for m in (pltpu.VMEM, pltpu.HBM, pl.ANY))
         sem = pltpu.SemaphoreType.DMA
         chunk = (k, LANES)
-        gram = (k // 2, 2 * k)
+        gram = (k // 4, 2 * k)
         by_rows, by_cols = jax.ShapeDtypeStruct((k, rows), F32), jax.ShapeDtypeStruct((k, cols), F32)
         outs = pl.pallas_call(
             functools.partial(kernel, n_s, n_t),
-            out_shape=(by_rows, by_cols, by_rows, by_cols, jax.ShapeDtypeStruct((k, k), F32)),
+            out_shape=(by_rows, by_cols, by_rows, by_cols),
             in_specs=[hbm, hbm],
-            out_specs=(vmem,) * 5,
+            out_specs=(vmem,) * 4,
             scratch_shapes=[
                 pltpu.VMEM((rows, cols), BF16),
                 pltpu.VMEM((k, cols), F32),
@@ -375,35 +391,35 @@
                 pltpu.VMEM((2, n_z, *chunk), F32),
                 pltpu.VMEM((2, n_z, *chunk), F32),
                 pltpu.VMEM((2, 2, n_z, *chunk), F32),
-                pltpu.VMEM((3, k, cols), F32),
+                pltpu.VMEM((4, k, cols), F32),
                 pltpu.VMEM((k, cols), F32),
                 pltpu.VMEM((k, rows), F32),
                 pltpu.VMEM((k // 2, LANES), F32),
                 pltpu.VMEM((k // 2, LANES), F32),
                 pltpu.VMEM((3, k, k), F32),
                 pltpu.VMEM((k, 2 * k), F32),
-                pltpu.VMEM((3, *gram), F32),
+                pltpu.VMEM((3, 2, *gram), F32),
+                pltpu.VMEM((2, *gram), F32),
                 pltpu.VMEM((n_t, *gram), F32),
                 pltpu.VMEM((2, n_z, *gram), F32),
-                pltpu.VMEM((2, *gram), F32),
-                pltpu.VMEM((2, *gram), F32),
+                pltpu.VMEM((3, 2, *gram), F32),
                 sem((math.isqrt(n_t),)), sem,
                 sem((2, 2)), sem((2, 2)), sem((2, 2)), sem((2, 2)),
                 sem((2, 2, n_g)), sem((2, 2, n_g)),
                 sem((2, 2)), sem((2, 2)), sem((2, 2)), sem((2, 2)), sem((2, 2)), sem((2, 2)),
-                sem((3,)), sem((3,)), sem((2,)), sem((2,)),
+                sem((2,)), sem((2,)), sem((3,)), sem((3,)), sem((3,)), sem((3,)),
             ],
             compiler_params=pltpu.CompilerParams(
                 collective_id=0, has_side_effects=True, vmem_limit_bytes=48 * 2**20
             ),
             name="range_finder",
-        )(traffic, sketch.T)
+        )(traffic, pltpu.with_memory_space_constraint(sketch.T, pltpu.HBM))
         first, back, basis, proj = pl.pallas_call(
             finish,
             out_shape=(by_rows, by_cols, by_rows, by_cols),
-            in_specs=[anywhere] * 3 + [vmem] * 2,
-            out_specs=(anywhere,) * 3 + (vmem,),
-            scratch_shapes=[sem((3,))],
+            in_specs=[anywhere] * 4,
+            out_specs=(anywhere,) * 4,
+            scratch_shapes=[sem((4,))],
             compiler_params=pltpu.CompilerParams(vmem_limit_bytes=8 * 2**20),
             name="finish",
         )(*outs)

time: 87.1 us -> 84.4 us (0.969)
  Pallas kernels: 85.1 us -> 83.5 us
  local copies, waits for them, and re-layouts: 1.03 us -> 0 us
    unnamed x2 -> x0, local copies, waits for them, and re-layouts: 1.03 us -> none
    pallas_call x1, Pallas kernels: 83.2 us -> 82.2 us  [local(): pl.pallas_call(functools.partial(kernel, n_s, n_t), out_shape=(by_rows, b...]
where the time goes in v3:
time: 84.4 us; the launch traced here: 84.3 us
  Pallas kernels  83.5 us (99%)
    pallas_call x1, Pallas kernels, local(): pl.pallas_call(functools.partial(kernel, n_s, n_t), out_shape=(by_rows, b...  82.2 us

profile of v3, /device:TPU:1, one launch (start us, length us, event | category | flops | bytes accessed | tf_op | source)
XLA Modules:
  0.0 84.3 jit_solution(14417439903926823024)
XLA Ops:
  0.6 82.2 %range_finder.1 = (f32[64,2048]{1,0:T(8,128)S(1)}, f32[64,2048]{1,0:T(8,128)S(1)}, f32[64,2048]{1,0:T(8,128)S(1)}, f32[64,2048]{1,0:T(8,128)S(1)}) custom-call(bf16[2048,2048]{1,0:T(8,128)(2,1)} %a_hbm.1, f32[64,2048]{1,0:T(8,128)} %bitcast.4), custom_call_target="tpu_custom_call" | custom-call | tf_op jit(solution)/shard_map/range_finder/pallas_call | solution.py:377
  82.8 1.3 %finish.1 = (f32[64,2048]{1,0:T(8,128)}, f32[64,2048]{1,0:T(8,128)}, f32[64,2048]{1,0:T(8,128)}, f32[64,2048]{1,0:T(8,128)}) custom-call(f32[64,2048]{1,0:T(8,128)S(1)} %get-tuple-element.12.refs_0_, f32[64,2048]{1,0:T(8,128)S(1)} %get-tuple-element.13.refs_1_, f32[64,2048]{1,0:T(8,128)S(1)} %get-tuple-element.14.refs_2_, ...), custom_call_target="tpu_custom_call" | custom-call | tf_op jit(solution)/shard_map/finish/pallas_call | solution.py:417

commit v4 on v3

--- a/solution.py
+++ b/solution.py
@@ -12,7 +12,7 @@
 HIGHEST = lax.Precision.HIGHEST
 MESH = pl.DeviceIdType.MESH
 LANES = 128
-PANEL = 8
+PANEL = 16
 NN = (((1,), (0,)), ((), ()))
 NT = (((1,), (1,)), ((), ()))
 
@@ -88,22 +88,26 @@
     def join(acc):
         return acc[:k_half] + (acc[k_half : 2 * k_half] + acc[2 * k_half : 3 * k_half])
 
-    def tm_product(stage, hs, between=None, ready=None):
+    def tm_multiply(stage, hs, dy):
+        acc = lax.dot_general(terms(*hs), a[tm_block(dy), :], NT, preferred_element_type=F32)
+        for h in hs:
+            val = join(acc[3 * (h - hs[0]) * k_half :])
+            for e in range(n_x):
+                tm_part[stage, tm_y[dy] * n_x + e, halves[h], :] = val[:, e * LANES : (e + 1) * LANES]
+
+    def tm_send(stage, h, dy):
+        for dx in far_first(n_x):
+            if (dy, dx) != (0, 0):
+                to = tm_to[dy, dx]
+                remote(
+                    tm_part.at[stage, to, halves[h], :], tm_in.at[stage, t, halves[h], :],
+                    tm_rs_s.at[stage, h], tm_rs_r.at[stage, h], s, to,
+                ).start()
+
+    def tm_product(stage, h, between=None):
         for i, dy in enumerate(far_first(n_y)):
-            if ready is not None:
-                ready(dy)
-            acc = lax.dot_general(terms(*hs), a[tm_block(dy), :], NT, preferred_element_type=F32)
-            for h in hs:
-                val = join(acc[3 * (h - hs[0]) * k_half :])
-                for e in range(n_x):
-                    tm_part[stage, tm_y[dy] * n_x + e, halves[h], :] = val[:, e * LANES : (e + 1) * LANES]
-                for dx in far_first(n_x):
-                    if (dy, dx) != (0, 0):
-                        to = tm_to[dy, dx]
-                        remote(
-                            tm_part.at[stage, to, halves[h], :], tm_in.at[stage, t, halves[h], :],
-                            tm_rs_s.at[stage, h], tm_rs_r.at[stage, h], s, to,
-                        ).start()
+            tm_multiply(stage, (h,), dy)
+            tm_send(stage, h, dy)
             if between and i == min(between[0], n_y - 1):
                 between[1]()
 
@@ -250,16 +254,19 @@
             work[pl.ds(k_half + c * k_quarter, k_quarter), :k_all] = packed[c, :, k_all:]
         v = work[...]
         for j in range(0, k_all, PANEL):
+            below = lax.broadcasted_iota(jnp.int32, v.shape, 0)
             col = [jnp.broadcast_to(v[:, j + m : j + m + 1], v.shape) for m in range(PANEL)]
-            line = [v[j + m : j + m + 1, :] for m in range(PANEL)]
+            line = [v[m : m + 1, :] for m in range(PANEL)]
             for m in range(PANEL):
-                factor = jnp.where(row > j + m, col[m] * (1.0 / col[m][j + m : j + m + 1, :]), 0.0)
+                factor = jnp.where(below > m, col[m] * (1.0 / col[m][m : m + 1, :]), 0.0)
                 for n in range(m + 1, PANEL):
-                    line[n] = line[n] - factor[j + n : j + n + 1, :] * line[m]
-                    col[n] = col[n] - factor * col[n][j + m : j + m + 1, :]
+                    line[n] = line[n] - factor[n : n + 1, :] * line[m]
+                    col[n] = col[n] - factor * col[n][m : m + 1, :]
                 v = v - factor * line[m]
-        diag = jnp.sum(jnp.where(lane == row, v, 0.0), axis=1, keepdims=True)
-        invs[i] = (v * lax.rsqrt(diag))[:, k_all:]
+            done, v = v[:PANEL], v[PANEL:]
+            mine = (lane == row + j)[:PANEL]
+            diag = jnp.sum(jnp.where(mine, done, 0.0), axis=1, keepdims=True)
+            invs[i, j : j + PANEL, :] = (done * lax.rsqrt(diag))[:, k_all:]
 
     def apply_a(i, low):
         return exact(invs[i, :k_half, :k_half], low)
@@ -271,12 +278,13 @@
     for h in range(2):
         split(sketch[halves[h], :], h, slice(None))
 
-    def ready(dy):
+    for dy in far_first(n_y):
         a_copies[dy].wait()
-        if dy == far_first(n_y)[0]:
-            pl.semaphore_wait(barrier, len(greeted))
-
-    tm_product(0, (0, 1), ready=ready)
+        tm_multiply(0, (0, 1), dy)
+    pl.semaphore_wait(barrier, len(greeted))
+    for h in range(2):
+        for dy in far_first(n_y):
+            tm_send(0, h, dy)
     for h in range(2):
         tm_gather(0, h, tm_sum(0, h))
     tm_take(0, 0, flats.at[0])
@@ -284,44 +292,36 @@
     z_product(0, 0)
     tm_take(0, 1, flats.at[0])
     z_both(0, 0, 0)
-    z_product(0, 1, (2, lambda: z_gather(0, 0, z_sum(0, 0))))
+    z_product(0, 1)
     z_both(0, 1, 0)
+    z_gather(0, 0, z_sum(0, 0))
     gram_z_send(0, flats.at[0])
     gram_z_pair(0)
     z_gather(0, 1, z_sum(0, 1))
     z_forward(0, 0)
     z_take(0, 0, flats.at[1])
-
-    def last_of_back():
-        gram_z_middle(0)
-        z_forward(0, 1)
-
-    tm_product(1, (0,), (2, last_of_back))
+    gram_z_middle(0)
+
+    tm_product(1, 0, (2, lambda: z_forward(0, 1)))
     invert(0, gram_end(0))
     z_take(0, 1, flats.at[1])
-
-    def tm_first_half():
-        tm_low[...] = tm_sum(1, 0)
-        tm_gather(1, 0, apply_a(0, tm_low[...]))
-
-    tm_product(1, (1,), (0, tm_first_half))
+    tm_product(1, 1)
+    tm_low[...] = tm_sum(1, 0)
+    tm_gather(1, 0, apply_a(0, tm_low[...]))
     back_flat[...] = exact(invs[0], flats[1])
     gram_tm_send(1, back_flat)
     first_out[...] = (rows_total**0.5) * exact(invs[0], flats[0])
     tm_gather(1, 1, apply_b(0, tm_low[...], tm_sum(1, 1)))
     tm_take(1, 0, flats.at[2])
 
-    z_product(1, 0, (2, lambda: gram_tm_middle(1)))
+    z_product(1, 0, (1, lambda: gram_tm_middle(1)))
     z_both(1, 0, 0)
     invert(1, gram_end(1))
     tm_take(1, 1, flats.at[2])
-
-    def z_first_half():
-        z_low[...] = z_sum(1, 0)
-        z_gather(1, 0, apply_a(1, z_low[...]))
-
-    z_product(1, 1, (1, z_first_half))
+    z_product(1, 1)
     z_both(1, 1, 0)
+    z_low[...] = z_sum(1, 0)
+    z_gather(1, 0, apply_a(1, z_low[...]))
     basis_flat[...] = exact(invs[1], flats[2])
     gram_z_send(2, basis_flat)
     gram_z_pair(2)

time: 84.4 us -> 84 us (level)
  no operation moved by 1% of the time
where the time goes in v4:
time: 84 us; the launch traced here: 83.9 us
  Pallas kernels  83.1 us (99%)
    pallas_call x1, Pallas kernels, local(): pl.pallas_call(functools.partial(kernel, n_s, n_t), out_shape=(by_rows, b...  81.7 us

profile of v4, /device:TPU:1, one launch (start us, length us, event | category | flops | bytes accessed | tf_op | source)
XLA Modules:
  0.0 83.9 jit_solution(3774886200195015987)
XLA Ops:
  0.6 81.7 %range_finder.1 = (f32[64,2048]{1,0:T(8,128)S(1)}, f32[64,2048]{1,0:T(8,128)S(1)}, f32[64,2048]{1,0:T(8,128)S(1)}, f32[64,2048]{1,0:T(8,128)S(1)}) custom-call(bf16[2048,2048]{1,0:T(8,128)(2,1)} %a_hbm.1, f32[64,2048]{1,0:T(8,128)} %bitcast.4), custom_call_target="tpu_custom_call" | custom-call | tf_op jit(solution)/shard_map/range_finder/pallas_call | solution.py:377
  82.4 1.3 %finish.1 = (f32[64,2048]{1,0:T(8,128)}, f32[64,2048]{1,0:T(8,128)}, f32[64,2048]{1,0:T(8,128)}, f32[64,2048]{1,0:T(8,128)}) custom-call(f32[64,2048]{1,0:T(8,128)S(1)} %get-tuple-element.12.refs_0_, f32[64,2048]{1,0:T(8,128)S(1)} %get-tuple-element.13.refs_1_, f32[64,2048]{1,0:T(8,128)S(1)} %get-tuple-element.14.refs_2_, ...), custom_call_target="tpu_custom_call" | custom-call | tf_op jit(solution)/shard_map/finish/pallas_call | solution.py:417

commit v5 on v4

--- a/solution.py
+++ b/solution.py
@@ -27,7 +27,7 @@
 
 def kernel(
     n_s, n_t, a_hbm, sketch_hbm, first_out, back_out, basis_out, proj_out,
-    a, sketch, lhs, tm_part, tm_in, tm_full, z_part, sib_in, z_send, z_in, z_full, flats, back_flat, basis_flat, tm_low, z_low, invs, work,
+    a, a_turned, sketch, lhs, tm_part, tm_in, tm_full, z_part, sib_in, z_send, z_in, z_full, flats, back_flat, basis_flat, tm_low, z_low, invs, work,
     g_out, g_pair, g_tm, g_z, g_sum,
     a_sem, s_sem, tm_rs_s, tm_rs_r, tm_ag_s, tm_ag_r, sib_s, sib_r, z_rs_s, z_rs_r, z_ag_s, z_ag_r, fw_s, fw_r,
     gp_s, gp_r, g_s, g_r, gs_s, gs_r,
@@ -89,7 +89,10 @@
         return acc[:k_half] + (acc[k_half : 2 * k_half] + acc[2 * k_half : 3 * k_half])
 
     def tm_multiply(stage, hs, dy):
-        acc = lax.dot_general(terms(*hs), a[tm_block(dy), :], NT, preferred_element_type=F32)
+        if stage == 0:
+            acc = lax.dot_general(terms(*hs), a[tm_block(dy), :], NT, preferred_element_type=F32)
+        else:
+            acc = lax.dot_general(terms(*hs), a_turned[:, tm_block(dy)], NN, preferred_element_type=F32)
         for h in hs:
             val = join(acc[3 * (h - hs[0]) * k_half :])
             for e in range(n_x):
@@ -285,25 +288,31 @@
     for h in range(2):
         for dy in far_first(n_y):
             tm_send(0, h, dy)
+
+    def turn(i, carry):
+        block = pl.ds(pl.multiple_of(i * 2 * LANES, 2 * LANES), 2 * LANES)
+        a_turned[:, block] = a[block, :].T
+        return carry
+
+    lax.fori_loop(0, rows // (2 * LANES), turn, 0)
     for h in range(2):
         tm_gather(0, h, tm_sum(0, h))
     tm_take(0, 0, flats.at[0])
 
     z_product(0, 0)
     tm_take(0, 1, flats.at[0])
+    gram_z_send(0, flats.at[0])
     z_both(0, 0, 0)
-    z_product(0, 1)
+    z_product(0, 1, (0, lambda: gram_z_pair(0)))
     z_both(0, 1, 0)
     z_gather(0, 0, z_sum(0, 0))
-    gram_z_send(0, flats.at[0])
-    gram_z_pair(0)
+    gram_z_middle(0)
     z_gather(0, 1, z_sum(0, 1))
+    invert(0, gram_end(0))
     z_forward(0, 0)
     z_take(0, 0, flats.at[1])
-    gram_z_middle(0)
 
     tm_product(1, 0, (2, lambda: z_forward(0, 1)))
-    invert(0, gram_end(0))
     z_take(0, 1, flats.at[1])
     tm_product(1, 1)
     tm_low[...] = tm_sum(1, 0)
@@ -381,6 +390,7 @@
             out_specs=(vmem,) * 4,
             scratch_shapes=[
                 pltpu.VMEM((rows, cols), BF16),
+                pltpu.VMEM((cols, rows), BF16),
                 pltpu.VMEM((k, cols), F32),
                 pltpu.VMEM((3 * k, cols), BF16),
                 pltpu.VMEM((2, n_t, *chunk), F32),

time: 84 us -> 81.3 us (0.968)
  Pallas kernels: 83.1 us -> 80.4 us
    pallas_call x1, Pallas kernels: 81.7 us -> 79.1 us  [local(): pl.pallas_call(functools.partial(kernel, n_s, n_t), out_shape=(by_rows, b...]
where the time goes in v5:
time: 81.3 us; the launch traced here: 81.2 us
  Pallas kernels  80.4 us (99%)
  between operations  0.82 us (1%)
    pallas_call x1, Pallas kernels, local(): pl.pallas_call(functools.partial(kernel, n_s, n_t), out_shape=(by_rows, b...  79.1 us

profile of v5, /device:TPU:1, one launch (start us, length us, event | category | flops | bytes accessed | tf_op | source)
XLA Modules:
  0.0 81.2 jit_solution(14549390129323244504)
XLA Ops:
  0.6 79.1 %range_finder.1 = (f32[64,2048]{1,0:T(8,128)S(1)}, f32[64,2048]{1,0:T(8,128)S(1)}, f32[64,2048]{1,0:T(8,128)S(1)}, f32[64,2048]{1,0:T(8,128)S(1)}) custom-call(bf16[2048,2048]{1,0:T(8,128)(2,1)} %a_hbm.1, f32[64,2048]{1,0:T(8,128)} %bitcast.4), custom_call_target="tpu_custom_call" | custom-call | tf_op jit(solution)/shard_map/range_finder/pallas_call | solution.py:386
  79.7 1.3 %finish.1 = (f32[64,2048]{1,0:T(8,128)}, f32[64,2048]{1,0:T(8,128)}, f32[64,2048]{1,0:T(8,128)}, f32[64,2048]{1,0:T(8,128)}) custom-call(f32[64,2048]{1,0:T(8,128)S(1)} %get-tuple-element.12.refs_0_, f32[64,2048]{1,0:T(8,128)S(1)} %get-tuple-element.13.refs_1_, f32[64,2048]{1,0:T(8,128)S(1)} %get-tuple-element.14.refs_2_, ...), custom_call_target="tpu_custom_call" | custom-call | tf_op jit(solution)/shard_map/finish/pallas_call | solution.py:427

commit v6 on v5

--- a/solution.py
+++ b/solution.py
@@ -261,7 +261,7 @@
             col = [jnp.broadcast_to(v[:, j + m : j + m + 1], v.shape) for m in range(PANEL)]
             line = [v[m : m + 1, :] for m in range(PANEL)]
             for m in range(PANEL):
-                factor = jnp.where(below > m, col[m] * (1.0 / col[m][m : m + 1, :]), 0.0)
+                factor = jnp.where(below > m, col[m], 0.0) * (1.0 / col[m][m : m + 1, :])
                 for n in range(m + 1, PANEL):
                     line[n] = line[n] - factor[n : n + 1, :] * line[m]
                     col[n] = col[n] - factor * col[n][m : m + 1, :]
@@ -324,8 +324,9 @@
     tm_take(1, 0, flats.at[2])
 
     z_product(1, 0, (1, lambda: gram_tm_middle(1)))
+    packed = gram_end(1)
     z_both(1, 0, 0)
-    invert(1, gram_end(1))
+    invert(1, packed)
     tm_take(1, 1, flats.at[2])
     z_product(1, 1)
     z_both(1, 1, 0)

time: 81.3 us -> 81.3 us (level)
  no operation moved by 1% of the time
where the time goes in v6:
time: 81.3 us; the launch traced here: 81.2 us
  Pallas kernels  80.4 us (99%)
  between operations  0.82 us (1%)
    pallas_call x1, Pallas kernels, local(): pl.pallas_call(functools.partial(kernel, n_s, n_t), out_shape=(by_rows, b...  79.1 us

profile of v6, /device:TPU:1, one launch (start us, length us, event | category | flops | bytes accessed | tf_op | source)
XLA Modules:
  0.0 81.2 jit_solution(3336170273422120862)
XLA Ops:
  0.6 79.1 %range_finder.1 = (f32[64,2048]{1,0:T(8,128)S(1)}, f32[64,2048]{1,0:T(8,128)S(1)}, f32[64,2048]{1,0:T(8,128)S(1)}, f32[64,2048]{1,0:T(8,128)S(1)}) custom-call(bf16[2048,2048]{1,0:T(8,128)(2,1)} %a_hbm.1, f32[64,2048]{1,0:T(8,128)} %bitcast.4), custom_call_target="tpu_custom_call" | custom-call | tf_op jit(solution)/shard_map/range_finder/pallas_call | solution.py:387
  79.7 1.3 %finish.1 = (f32[64,2048]{1,0:T(8,128)}, f32[64,2048]{1,0:T(8,128)}, f32[64,2048]{1,0:T(8,128)}, f32[64,2048]{1,0:T(8,128)}) custom-call(f32[64,2048]{1,0:T(8,128)S(1)} %get-tuple-element.12.refs_0_, f32[64,2048]{1,0:T(8,128)S(1)} %get-tuple-element.13.refs_1_, f32[64,2048]{1,0:T(8,128)S(1)} %get-tuple-element.14.refs_2_, ...), custom_call_target="tpu_custom_call" | custom-call | tf_op jit(solution)/shard_map/finish/pallas_call | solution.py:428

commit v7 on v6

--- a/solution.py
+++ b/solution.py
@@ -248,15 +248,17 @@
             total = total + g_tm[k]
         gram_swap(i, total)
 
-    def invert(i, packed):
+    def invert(i, packed, start=0, stop=None):
+        stop = k_all if stop is None else stop
         lane = lax.broadcasted_iota(jnp.int32, (k_all, 2 * k_all), 1)
         row = lax.broadcasted_iota(jnp.int32, (k_all, 2 * k_all), 0)
-        work[...] = jnp.where(lane == row + k_all, 1.0, 0.0).astype(F32)
-        for c in range(2):
-            work[pl.ds(c * k_quarter, k_quarter), :k_all] = packed[c, :, :k_all]
-            work[pl.ds(k_half + c * k_quarter, k_quarter), :k_all] = packed[c, :, k_all:]
-        v = work[...]
-        for j in range(0, k_all, PANEL):
+        if packed is not None:
+            work[...] = jnp.where(lane == row + k_all, 1.0, 0.0).astype(F32)
+            for c in range(2):
+                work[pl.ds(c * k_quarter, k_quarter), :k_all] = packed[c, :, :k_all]
+                work[pl.ds(k_half + c * k_quarter, k_quarter), :k_all] = packed[c, :, k_all:]
+        v = work[start:, :]
+        for j in range(start, stop, PANEL):
             below = lax.broadcasted_iota(jnp.int32, v.shape, 0)
             col = [jnp.broadcast_to(v[:, j + m : j + m + 1], v.shape) for m in range(PANEL)]
             line = [v[m : m + 1, :] for m in range(PANEL)]
@@ -270,6 +272,8 @@
             mine = (lane == row + j)[:PANEL]
             diag = jnp.sum(jnp.where(mine, done, 0.0), axis=1, keepdims=True)
             invs[i, j : j + PANEL, :] = (done * lax.rsqrt(diag))[:, k_all:]
+        if stop < k_all:
+            work[stop:, :] = v
 
     def apply_a(i, low):
         return exact(invs[i, :k_half, :k_half], low)
@@ -326,12 +330,13 @@
     z_product(1, 0, (1, lambda: gram_tm_middle(1)))
     packed = gram_end(1)
     z_both(1, 0, 0)
-    invert(1, packed)
+    invert(1, packed, 0, k_half)
     tm_take(1, 1, flats.at[2])
     z_product(1, 1)
     z_both(1, 1, 0)
     z_low[...] = z_sum(1, 0)
     z_gather(1, 0, apply_a(1, z_low[...]))
+    invert(1, None, k_half)
     basis_flat[...] = exact(invs[1], flats[2])
     gram_z_send(2, basis_flat)
     gram_z_pair(2)

time: 81.3 us -> 80.5 us (level)
  no operation moved by 1% of the time
where the time goes in v7:
time: 80.5 us; the launch traced here: 80.4 us
  Pallas kernels  79.6 us (99%)
  between operations  0.82 us (1%)
    pallas_call x1, Pallas kernels, local(): pl.pallas_call(functools.partial(kernel, n_s, n_t), out_shape=(by_rows, b...  78.3 us

profile of v7, /device:TPU:1, one launch (start us, length us, event | category | flops | bytes accessed | tf_op | source)
XLA Modules:
  0.0 80.4 jit_solution(18392073600372766445)
XLA Ops:
  0.6 78.3 %range_finder.1 = (f32[64,2048]{1,0:T(8,128)S(1)}, f32[64,2048]{1,0:T(8,128)S(1)}, f32[64,2048]{1,0:T(8,128)S(1)}, f32[64,2048]{1,0:T(8,128)S(1)}) custom-call(bf16[2048,2048]{1,0:T(8,128)(2,1)} %a_hbm.1, f32[64,2048]{1,0:T(8,128)} %bitcast.4), custom_call_target="tpu_custom_call" | custom-call | tf_op jit(solution)/shard_map/range_finder/pallas_call | solution.py:392
  78.9 1.3 %finish.1 = (f32[64,2048]{1,0:T(8,128)}, f32[64,2048]{1,0:T(8,128)}, f32[64,2048]{1,0:T(8,128)}, f32[64,2048]{1,0:T(8,128)}) custom-call(f32[64,2048]{1,0:T(8,128)S(1)} %get-tuple-element.12.refs_0_, f32[64,2048]{1,0:T(8,128)S(1)} %get-tuple-element.13.refs_1_, f32[64,2048]{1,0:T(8,128)S(1)} %get-tuple-element.14.refs_2_, ...), custom_call_target="tpu_custom_call" | custom-call | tf_op jit(solution)/shard_map/finish/pallas_call | solution.py:433
